TPU v7x, 32 devices: a whole 2x2x4 slice. The times are simulated.
32 devices in a mesh: groups: 2 (over x), gx: 16 (over z, y, core).
Axes of the slice: x: 2, y: 2, z: 4, core: 2. Of those that a mesh axis runs over, the one named last changes fastest.
Arguments:
- hidden: bfloat16 [39936, 768], P('gx', 'groups'), parts along dimension 1, may hold values from -6 to 6
- residual: bfloat16 [16384, 768], P('gx', 'groups'), parts along dimension 1, may hold values from -120 to 120
- w_down: bfloat16 [16, 19968, 2048], P('gx'), may hold values from -0.03125 to 0.03125
- gain: bfloat16 [16384], P('gx'), may hold values from 0.099609375 to 1.8984375
- w_qkv: bfloat16 [16, 2048, 5120], P('gx'), may hold values from -0.046875 to 0.046875
Outputs:
- stream: bfloat16 [16384, 768], P('gx', 'groups'), parts along dimension 1
- qkv: bfloat16 [10240, 768], P('gx', 'groups'), parts along dimension 1
There are 2 independent parts, one for each index of `groups`. A program takes and returns all parts, laid end to end along the dimension named above; an argument that names none is the same for every part. Nothing has to cross between parts.
All inputs are finite; a program needn't handle non-finite values.
Results may differ from a plain program's by a relative error of at most 0.0058.
Values may be sent and summed in bfloat16 or wider, within the bound.
A program may use at most 192 MiB of HBM per device.

v0:
```python
import jax
import jax.numpy as jnp
from jax import lax
from jax.sharding import PartitionSpec as P

D = 16384
XS = 8


def swapped(block, axis, stride):
    count = lax.axis_size(axis)
    route = []
    for low in range(count):
        high = low | 1 << stride
        if high != low and high < count:
            route += [(low, high), (high, low)]
    return lax.ppermute(block, axis, route)


def for_sending(value):
    return jax.tree.map(lambda a: a.astype(jnp.bfloat16) if a.dtype == jnp.float32 else a, value)


def bit_of(dev_index, position):
    return dev_index // 2**position % 2


def collect_bits(current, positions, dev_index, send_fn):
    for position in positions:
        received = send_fn(current, position)
        high_bit = bit_of(dev_index, position) == 1
        current = jax.tree.map(
            lambda own_part, their_part: jnp.where(
                high_bit,
                jnp.concatenate([their_part, own_part], 0),
                jnp.concatenate([own_part, their_part], 0),
            ),
            current,
            received,
        )
    return current


def halve_bits(partial_value, first_bit, bit_count, bit_order, dev_index, send_fn):
    trailing = partial_value.shape[1:]
    shaped = partial_value.reshape(
        (2,) * bit_count + (partial_value.shape[0] // 2**bit_count,) + trailing
    )
    remaining = list(range(bit_count - 1, -1, -1))
    for relative in bit_order:
        axis_pos = sum([1 for other in remaining if other > relative])
        high_bit = bit_of(dev_index, first_bit + relative)
        retained = lax.dynamic_index_in_dim(shaped, high_bit, axis_pos, keepdims=False)
        outgoing = lax.dynamic_index_in_dim(shaped, 1 - high_bit, axis_pos, keepdims=False)
        shaped = retained + send_fn(outgoing, first_bit + relative)
        remaining = [other for other in remaining if other != relative]
    return shaped


def on_device(hidden, residual, w_down, gain, w_qkv):
    dev_index = lax.axis_index("gx")
    y_bits = (lax.axis_size("gx") // XS).bit_length() - 1
    x_bits = XS.bit_length() - 1
    x_positions = list(range(y_bits, y_bits + x_bits))
    y_positions = list(range(y_bits))
    tile_down = w_down[0]
    tile_qkv = w_qkv[0]
    gathered = collect_bits(
        hidden, x_positions, dev_index, lambda current, position: swapped(current, "gx", position)
    )
    partial_down = lax.dot_general(
        tile_down, gathered, (((0,), (0,)), ((), ())), preferred_element_type=jnp.float32
    )
    down_order = list(range(y_bits - 1, -1, -1))
    down = halve_bits(
        partial_down,
        0,
        y_bits,
        down_order,
        dev_index,
        lambda current, position: swapped(current, "gx", position),
    )
    stream = (residual.astype(jnp.float32) + down).astype(jnp.bfloat16)
    block_stream, block_gain = collect_bits(
        (stream, gain),
        y_positions,
        dev_index,
        lambda current, position: jax.tree.map(
            lambda part, own: part.astype(own.dtype),
            swapped(for_sending(current), "gx", position),
            current,
        ),
    )
    block_values = block_stream.astype(jnp.float32)
    sumsq = jnp.sum(block_values * block_values, axis=0)
    for position in x_positions:
        sumsq = sumsq + swapped(sumsq, "gx", position)
    inv_rms = lax.rsqrt(sumsq / D + 1e-05)
    block_normed = (
        block_values * block_gain.astype(jnp.float32)[:, None] * inv_rms[None, :]
    ).astype(jnp.bfloat16)
    partial_qkv = lax.dot_general(
        tile_qkv, block_normed, (((0,), (0,)), ((), ())), preferred_element_type=jnp.float32
    )
    qkv_order = list(range(x_bits - 1, -1, -1))
    qkv = halve_bits(
        partial_qkv,
        y_bits,
        x_bits,
        qkv_order,
        dev_index,
        lambda current, position: swapped(current, "gx", position),
    )
    return (stream, qkv.astype(jnp.bfloat16))


def solution(mesh):
    placed = (
        P("gx", "groups"),
        P("gx", "groups"),
        P("gx", None, None),
        P("gx"),
        P("gx", None, None),
    )
    return jax.shard_map(
        on_device,
        mesh=mesh,
        in_specs=placed,
        out_specs=(P("gx", "groups"), P("gx", "groups")),
        check_vma=False,
    )
```

profile of v0, /device:TPU:0, one launch (start us, length us, event | category | flops | bytes accessed | tf_op | source)
XLA Modules:
  0.0 848.8 jit_solution(1088050198621588809)
XLA Ops:
  0.6 3.0 collective-permute-start
  3.7 42.0 %collective-permute-done = bf16[2496,384]{1,0:T(8,128)(2,1)S(1)} collective-permute-done((bf16[2496,384]{1,0:T(8,128)(2,1)}, bf16[2496,384]{1,0:T(8,128)(2,1)S(1)}, u32[]{:S(2)}, u32[]{:S(2)}) %collective-permute-start) | collective-permute-done | bytes 1916960 | tf_op jit(solution)/shard_map/ppermute | solution.py:17
  45.6 5.5 maximum_select_fusion.3
  51.1 1.8 collective-permute-start.1
  52.9 82.6 %collective-permute-done.1 = bf16[4992,384]{1,0:T(8,128)(2,1)} collective-permute-done((bf16[4992,384]{1,0:T(8,128)(2,1)}, bf16[4992,384]{1,0:T(8,128)(2,1)}, u32[]{:S(2)}, u32[]{:S(2)}) %collective-permute-start.1) | collective-permute-done | bytes 3833888 | tf_op jit(solution)/shard_map/ppermute | solution.py:17
  135.5 12.8 %maximum_select_fusion.2 = bf16[9984,384]{1,0:T(8,128)(2,1)} fusion(bf16[4992,384]{1,0:T(8,128)(2,1)} %maximum_select_fusion.3, bf16[4992,384]{1,0:T(8,128)(2,1)} %collective-permute-done.1, pred[]{:T(512)S(6)} %eq.22), kind=kLoop, calls=%fused_computation.11 | loop fusion | flops 34504704 | bytes 15335425 | tf_op jit(solution)/shard_map/jit(_where)/select_n | solution.py:33
  148.3 2.5 collective-permute-start.2
  150.7 328.3 %collective-permute-done.2 = bf16[9984,384]{1,0:T(8,128)(2,1)} collective-permute-done((bf16[9984,384]{1,0:T(8,128)(2,1)}, bf16[9984,384]{1,0:T(8,128)(2,1)}, u32[]{:S(2)}, u32[]{:S(2)}) %collective-permute-start.2) | collective-permute-done | bytes 7667744 | tf_op jit(solution)/shard_map/ppermute | solution.py:17
  479.1 51.4 %fusion.16 = f32[2048,384]{0,1:T(8,128)} fusion(bf16[1,19968,2048]{2,1,0:T(8,128)(2,1)} %param.7, bf16[9984,384]{1,0:T(8,128)(2,1)} %maximum_select_fusion.2, bf16[9984,384]{1,0:T(8,128)(2,1)} %collective-permute-done.2, pred[]{:T(512)S(6)} %eq.21), kind=kOutput, calls=%fused_computation.21 | convolution fusion | flops 31475957760 | bytes 100270080 | tf_op jit(solution)/shard_map/dot_general | solution.py:71
  530.4 4.4 reshape.41
  534.9 4.4 constant_dynamic-slice_fusion.3
  539.2 5.0 copy.8
  545.4 2.6 collective-permute-done.3
  548.0 1.8 fusion.21
  550.0 2.1 collective-permute-done.4
  552.8 1.2 collective-permute-start.6
  553.9 2.5 collective-permute-done.6
  556.7 3.3 collective-permute-done.7
  560.0 1.6 collective-permute-start.8
  561.6 2.9 collective-permute-done.8
  564.5 14.8 %fusion.10 = f32[5120,384]{0,1:T(8,128)} fusion(bf16[1,2048,5120]{2,1,0:T(8,128)(2,1)} %param.9, f32[384]{0:T(512)S(1)} %add_rsqrt_fusion, f32[2048]{0:T(1024)S(1)} %fusion.25, bf16[1024,384]{1,0:T(8,128)(2,1)S(1)} %fusion.21, bf16[1024,384]{1,0:T(8,128)(2,1)S(1)} %collective-permute-done.4, pred[]{:T(512)S(6)} %eq.24), kind=kOutput, calls=%fused_computation.12 | convolution fusion | flops 8063287296 | bytes 30418432 | tf_op jit(solution)/shard_map/dot_general | solution.py:102
  579.3 11.1 %reshape.42 = f32[2,2,2,640,384]{3,2,1,0,4:T(2,128)} reshape(f32[5120,384]{0,1:T(8,128)} %fusion.10) | data formatting | bytes 15728640 | tf_op jit(solution)/shard_map/reshape | solution.py:46
  590.4 5.4 dynamic-slice_bitcast_fusion
  595.8 1.6 collective-permute-start.9
  597.4 167.4 %collective-permute-done.9 = f32[2,2,640,384]{2,1,0,3:T(2,128)} collective-permute-done((f32[2,2,640,384]{2,1,0,3:T(2,128)}, f32[2,2,640,384]{2,1,0,3:T(2,128)}, u32[]{:S(2)}, u32[]{:S(2)}) %collective-permute-start.9) | collective-permute-done | bytes 3932192 | tf_op jit(solution)/shard_map/ppermute | solution.py:17
  764.9 5.4 bitcast_add_fusion
  770.2 2.6 constant_dynamic-slice_fusion.1
  772.8 4.7 copy.10
  777.5 3.2 copy.9
  780.8 41.3 %collective-permute-done.10 = f32[2,640,384]{2,1,0:T(8,128)} collective-permute-done((f32[2,640,384]{2,1,0:T(8,128)}, f32[2,640,384]{2,1,0:T(8,128)}, u32[]{:S(2)}, u32[]{:S(2)}) %collective-permute-start.10) | collective-permute-done | bytes 1966112 | tf_op jit(solution)/shard_map/ppermute | solution.py:17
  822.1 2.3 bitcast_add_fusion.1
  826.2 21.8 %collective-permute-done.11 = f32[640,384]{1,0:T(8,128)S(1)} collective-permute-done((f32[640,384]{1,0:T(8,128)}, f32[640,384]{1,0:T(8,128)S(1)}, u32[]{:S(2)}, u32[]{:S(2)}) %collective-permute-start.11) | collective-permute-done | bytes 983072 | tf_op jit(solution)/shard_map/ppermute | solution.py:17
  (21 shorter events, 4.8 us)
Async XLA Ops:
  0.6 45.0 %collective-permute-start = (bf16[2496,384]{1,0:T(8,128)(2,1)}, bf16[2496,384]{1,0:T(8,128)(2,1)S(1)}, u32[]{:S(2)}, u32[]{:S(2)}) collective-permute-start(bf16[2496,384]{1,0:T(8,128)(2,1)} %param.5), channel_id=1, source_target_pairs={{0,2},{2,0},{1,3},{3,1},{4,6},{6,4},{5,7},{7,5},{8,10},{10,8},{9,1... | collective-permute-start | bytes 5750792 | tf_op jit(solution)/shard_map/ppermute | solution.py:17
  51.1 84.3 %collective-permute-start.1 = (bf16[4992,384]{1,0:T(8,128)(2,1)}, bf16[4992,384]{1,0:T(8,128)(2,1)}, u32[]{:S(2)}, u32[]{:S(2)}) collective-permute-start(bf16[4992,384]{1,0:T(8,128)(2,1)} %maximum_select_fusion.3), channel_id=1, source_target_pairs={{0,4},{4,0},{1,5},{5,1},{2,6},{6,2},{3,7},{7,3},{8,12},{12,8},{9,1... | collective-permute-start | bytes 11501576 | tf_op jit(solution)/shard_map/ppermute | solution.py:17
  148.3 330.8 %collective-permute-start.2 = (bf16[9984,384]{1,0:T(8,128)(2,1)}, bf16[9984,384]{1,0:T(8,128)(2,1)}, u32[]{:S(2)}, u32[]{:S(2)}) collective-permute-start(bf16[9984,384]{1,0:T(8,128)(2,1)} %maximum_select_fusion.2), channel_id=1, source_target_pairs={{0,8},{8,0},{1,9},{9,1},{2,10},{10,2},{3,11},{11,3},{4,12},{12,4},... | collective-permute-start | bytes 23003144 | tf_op jit(solution)/shard_map/ppermute | solution.py:17
  539.2 5.0 copy-start
  544.2 3.8 collective-permute-start.3
  545.3 8.6 %copy-start.2 = (bf16[1024]{0:T(1024)(128)(2,1)S(1)}, bf16[1024]{0:T(1024)(128)(2,1)}, u32[]{:S(2)}) copy-start(bf16[1024]{0:T(1024)(128)(2,1)} %param.8) | copy-start | bytes 6148
  549.8 29.5 %copy-start.1 = (bf16[1024,384]{1,0:T(8,128)(2,1)}, bf16[1024,384]{1,0:T(8,128)(2,1)S(1)}, u32[]{:S(2)}) copy-start(bf16[1024,384]{1,0:T(8,128)(2,1)S(1)} %fusion.21) | copy-start | bytes 2359300
  549.8 2.4 collective-permute-start.4
  552.8 3.6 collective-permute-start.6
  553.9 7.7 collective-permute-start.5
  556.4 3.6 collective-permute-start.7
  560.0 4.5 collective-permute-start.8
  595.8 169.0 %collective-permute-start.9 = (f32[2,2,640,384]{2,1,0,3:T(2,128)}, f32[2,2,640,384]{2,1,0,3:T(2,128)}, u32[]{:S(2)}, u32[]{:S(2)}) collective-permute-start(f32[2,2,640,384]{2,1,0,3:T(2,128)} %dynamic-slice_bitcast_fusion), channel_id=1, source_target_pairs={{0,8},{8,0},{1,9},{9,1},{2,10},{10,2},{3,11},{11,3},{4,12},{12,4},... | collective-permute-start | bytes 11796488 | tf_op jit(solution)/shard_map/ppermute | solution.py:17
  777.5 44.6 %collective-permute-start.10 = (f32[2,640,384]{2,1,0:T(8,128)}, f32[2,640,384]{2,1,0:T(8,128)}, u32[]{:S(2)}, u32[]{:S(2)}) collective-permute-start(f32[2,640,384]{2,1,0:T(8,128)} %bitcast.40), channel_id=1, source_target_pairs={{0,4},{4,0},{1,5},{5,1},{2,6},{6,2},{3,7},{7,3},{8,12},{12,8},{9,1... | collective-permute-start | bytes 5898248 | tf_op jit(solution)/shard_map/ppermute | solution.py:17
  825.5 22.5 %collective-permute-start.11 = (f32[640,384]{1,0:T(8,128)}, f32[640,384]{1,0:T(8,128)S(1)}, u32[]{:S(2)}, u32[]{:S(2)}) collective-permute-start(f32[640,384]{1,0:T(8,128)} %dynamic-slice_bitcast_fusion.1), channel_id=1, source_target_pairs={{0,2},{2,0},{1,3},{3,1},{4,6},{6,4},{5,7},{7,5},{8,10},{10,8},{9,1... | collective-permute-start | bytes 2949128 | tf_op jit(solution)/shard_map/ppermute | solution.py:17
where the time goes:
time: 850 us; the launch traced here: 849 us
  waiting for transfers between devices  697 us (82%)
  matrix products  66.1 us (8%)
  local copies, waits for them, and re-layouts  43 us (5%)
  other arithmetic  29.3 us (3%)
  starting transfers between devices  12.9 us (2%)
    ppermute x12, waiting for transfers between devices, swapped(): return lax.ppermute(block, axis, route)  697 us
    dot_general x1, matrix products, on_device(): lax.dot_general(tile_down, gathered, (((0,), (0,)), ((), ())), preferred_...  51.4 us
    select_n x2, other arithmetic, collect_bits(): jnp.where(high_bit, jnp.concatenate([their_part, own_part], 0), jnp.conca...  18.3 us
  transfers between devices with their start and end apart: 12, of which 11 were waited for; matrix products, arithmetic and copies ran while one was open for 1% of the time, Pallas kernels for 0%

commit v1 on v0

--- a/solution.py
+++ b/solution.py
@@ -1,10 +1,15 @@
+import functools
+
 import jax
 import jax.numpy as jnp
 from jax import lax
+from jax.experimental import pallas as pl
+from jax.experimental.pallas import tpu as pltpu
 from jax.sharding import PartitionSpec as P
 
 D = 16384
 XS = 8
+MESH = pl.DeviceIdType.MESH
 
 
 def swapped(block, axis, stride):
@@ -57,7 +62,7 @@
     return shaped
 
 
-def on_device(hidden, residual, w_down, gain, w_qkv):
+def permuted(hidden, residual, w_down, gain, w_qkv):
     dev_index = lax.axis_index("gx")
     y_bits = (lax.axis_size("gx") // XS).bit_length() - 1
     x_bits = XS.bit_length() - 1
@@ -114,6 +119,455 @@
     return (stream, qkv.astype(jnp.bfloat16))
 
 
+def ring_position(tile, count):
+    odd = lax.rem(tile, 2)
+    step = tile // 2
+    return (1 - odd) * step + odd * (count - 1 - step)
+
+
+def ring_tile(position, count):
+    back = position // (count // 2)
+    return (1 - back) * (2 * position) + back * (2 * (count - 1 - position) + 1)
+
+
+def fused_kernel(
+    xs,
+    ys,
+    cuts,
+    width,
+    hidden,
+    residual,
+    w_down,
+    gain,
+    w_qkv,
+    stream_out,
+    qkv_out,
+    held,
+    res_buf,
+    down_buf,
+    qkv_buf,
+    acc,
+    acc_in,
+    feats,
+    sums,
+    pair_sums,
+    ring_sums,
+    out_msg,
+    in_msg,
+    own,
+    local_sem,
+    down_sem,
+    qkv_sem,
+    ring_send,
+    ring_recv,
+    acc_send,
+    acc_recv,
+    feat_send,
+    feat_recv,
+    psum_send,
+    psum_recv,
+    rsum_send,
+    rsum_recv,
+    msg_send,
+    msg_recv,
+):
+    me = lax.axis_index("gx")
+    tile, part = me // ys, lax.rem(me, ys)
+    place = ring_position(tile, xs)
+    rows = hidden.shape[0]
+    cut = rows // cuts
+    tokens = hidden.shape[1]
+    feat = residual.shape[0]
+    cols = qkv_out.shape[0]
+    half_ring = xs // 2
+    half = tokens // 2
+
+    def device_at(x, y):
+        return {"gx": x * ys + y}
+
+    def tile_at(direction, distance):
+        return ring_tile(lax.rem(place + (2 * direction - 1) * distance + xs, xs), xs)
+
+    ahead = [device_at(tile_at(1, 1), part), device_at(tile_at(0, 1), part)]
+
+    def arrival(direction, item):
+        piece = tile_at(direction, item // cuts + 1)
+        order = lax.rem(item, cuts)
+        return piece, order if direction == 0 else cuts - 1 - order
+
+    def window(piece, chunk):
+        return held.at[piece, pl.ds(pl.multiple_of(chunk * cut, cut), cut)]
+
+    def gather_copy(direction, item, piece, chunk, source):
+        return pltpu.make_async_remote_copy(
+            src_ref=source,
+            dst_ref=window(piece, chunk),
+            send_sem=ring_send.at[direction, item],
+            recv_sem=ring_recv.at[direction, item],
+            device_id=ahead[direction],
+            device_id_type=MESH,
+        )
+
+    def down_copy(slot, piece, chunk):
+        start = pl.multiple_of(piece * rows + chunk * cut, cut)
+        return pltpu.make_async_copy(
+            w_down.at[pl.ds(start, cut)], down_buf.at[slot], down_sem.at[slot]
+        )
+
+    def qkv_copy(owner):
+        return pltpu.make_async_copy(
+            w_qkv.at[:, pl.ds(owner * cols, cols)], qkv_buf.at[owner], qkv_sem.at[owner]
+        )
+
+    barrier = pltpu.get_barrier_semaphore()
+    for offset in range(1, xs):
+        pl.semaphore_signal(
+            barrier,
+            inc=1,
+            device_id=device_at(lax.rem(tile + offset, xs), part),
+            device_id_type=MESH,
+        )
+    for offset in range(1, ys):
+        pl.semaphore_signal(
+            barrier,
+            inc=1,
+            device_id=device_at(tile, lax.rem(part + offset, ys)),
+            device_id_type=MESH,
+        )
+    pl.semaphore_wait(barrier, xs - 1 + ys - 1)
+
+    arrivals = cuts * (half_ring - 1) + cuts // 2
+    for item in range(cuts):
+        for direction in range(2):
+            chunk = item if direction == 0 else cuts - 1 - item
+            gather_copy(
+                direction, item, tile, chunk, hidden.at[pl.ds(chunk * cut, cut)]
+            ).start()
+    own_copy = pltpu.make_async_copy(hidden, held.at[tile], local_sem.at[0])
+    own_copy.start()
+    res_copy = pltpu.make_async_copy(residual, res_buf, local_sem.at[1])
+    res_copy.start()
+    for lane in range(2):
+        down_copy(lane, tile, lane).start()
+    acc[...] = jnp.zeros_like(acc)
+    res_copy.wait()
+    acc[part] = res_buf[...].astype(jnp.float32).T
+    own_copy.wait()
+
+    def transposed(piece, chunk):
+        return held[piece, pl.ds(pl.multiple_of(chunk * cut, cut), cut), :].T
+
+    def add_block(block, base, first, first_slot, second, second_slot):
+        for start in range(0, feat, width):
+            at = pl.ds(pl.multiple_of(base + start, width), width)
+            acc[block, :, start : start + width] += jnp.dot(
+                first, down_buf[first_slot, :, at], preferred_element_type=jnp.float32
+            ) + jnp.dot(second, down_buf[second_slot, :, at], preferred_element_type=jnp.float32)
+
+    def own_pair(pair, carry):
+        slot = lax.rem(pair, 2) * 2
+        following = 2 - slot
+
+        @pl.when(pair + 1 < cuts // 2)
+        def _():
+            for lane in range(2):
+                down_copy(following + lane, tile, 2 * pair + 2 + lane).start()
+
+        @pl.when(pair + 1 == cuts // 2)
+        def _():
+            for lane in range(2):
+                down_copy(following + lane, *arrival(lane, 0)).start()
+
+        for lane in range(2):
+            down_copy(slot + lane, tile, 2 * pair + lane).wait()
+        first, second = transposed(tile, 2 * pair), transposed(tile, 2 * pair + 1)
+        for block in range(ys):
+            add_block(block, block * feat, first, slot, second, slot + 1)
+        return carry
+
+    lax.fori_loop(0, cuts // 2, own_pair, 0)
+    for owner in range(xs):
+        qkv_copy(owner).start()
+
+    def receive(item, forward):
+        for direction in range(2):
+            piece, chunk = arrival(direction, item)
+            gather_copy(direction, item, piece, chunk, window(piece, chunk)).wait_recv()
+            if forward:
+
+                @pl.when(item + cuts < arrivals)
+                def _():
+                    gather_copy(
+                        direction, item + cuts, piece, chunk, window(piece, chunk)
+                    ).start()
+
+    def weights_of(item, slot):
+        for lane in range(2):
+            down_copy(slot + lane, *arrival(lane, item)).wait()
+
+    def ring_pair(item, carry):
+        slot = lax.rem(item + cuts // 2, 2) * 2
+        following = 2 - slot
+        for lane in range(2):
+            down_copy(following + lane, *arrival(lane, item + 1)).start()
+        receive(item, True)
+        weights_of(item, slot)
+        first, second = transposed(*arrival(0, item)), transposed(*arrival(1, item))
+        for block in range(ys):
+            add_block(block, block * feat, first, slot, second, slot + 1)
+        return carry
+
+    lax.fori_loop(0, arrivals - 1, ring_pair, 0)
+
+    last = arrivals - 1
+    slot = (last + cuts // 2) % 2 * 2
+    receive(last, False)
+    weights_of(last, slot)
+    first, second = transposed(*arrival(0, last)), transposed(*arrival(1, last))
+    acc_copies = []
+    for offset in range(1, ys):
+        other = lax.rem(part + offset, ys)
+        add_block(other, other * feat, first, slot, second, slot + 1)
+        acc_copies.append(
+            pltpu.make_async_remote_copy(
+                src_ref=acc.at[other],
+                dst_ref=acc_in.at[offset - 1],
+                send_sem=acc_send.at[offset - 1],
+                recv_sem=acc_recv.at[offset - 1],
+                device_id=device_at(tile, other),
+                device_id_type=MESH,
+            )
+        )
+        acc_copies[-1].start()
+    add_block(part, part * feat, first, slot, second, slot + 1)
+    total = acc[part]
+    for copy in acc_copies:
+        copy.wait_recv()
+    for offset in range(1, ys):
+        total = total + acc_in[offset - 1]
+    values = total.astype(jnp.bfloat16).astype(jnp.float32)
+    acc[part] = values
+    feats[part] = (values * gain[...].astype(jnp.float32)).astype(jnp.bfloat16)
+    feat_copies = []
+    for offset in range(1, ys):
+        other = lax.rem(part + offset, ys)
+        feat_copies.append(
+            [
+                pltpu.make_async_remote_copy(
+                    src_ref=feats.at[sender],
+                    dst_ref=feats.at[sender],
+                    send_sem=feat_send.at[offset - 1],
+                    recv_sem=feat_recv.at[offset - 1],
+                    device_id=device_at(tile, other),
+                    device_id_type=MESH,
+                )
+                for sender in (part, lax.rem(part + ys - offset, ys))
+            ]
+        )
+        feat_copies[-1][0].start()
+
+    upright = acc[part].T
+    stream_out[...] = upright.astype(jnp.bfloat16)
+    sums[...] = jnp.broadcast_to(jnp.sum(upright * upright, axis=0, keepdims=True), sums.shape)
+    sum_copies = []
+    for offset in range(1, ys):
+        sum_copies.append(
+            pltpu.make_async_remote_copy(
+                src_ref=sums,
+                dst_ref=pair_sums.at[offset - 1],
+                send_sem=psum_send.at[offset - 1],
+                recv_sem=psum_recv.at[offset - 1],
+                device_id=device_at(tile, lax.rem(part + offset, ys)),
+                device_id_type=MESH,
+            )
+        )
+        sum_copies[-1].start()
+
+    for owner in range(xs):
+        qkv_copy(owner).wait()
+    for _, incoming in feat_copies:
+        incoming.wait_recv()
+
+    def project(owner, start, size):
+        result = jnp.dot(
+            feats[0, pl.ds(start, size), :],
+            qkv_buf[owner, :feat, :],
+            preferred_element_type=jnp.float32,
+        )
+        for block in range(1, ys):
+            result = result + jnp.dot(
+                feats[block, pl.ds(start, size), :],
+                qkv_buf[owner, block * feat : (block + 1) * feat, :],
+                preferred_element_type=jnp.float32,
+            )
+        return result
+
+    def message_copy(direction, index):
+        return pltpu.make_async_remote_copy(
+            src_ref=out_msg.at[direction, index],
+            dst_ref=in_msg.at[direction, index],
+            send_sem=msg_send.at[direction, index],
+            recv_sem=msg_recv.at[direction, index],
+            device_id=ahead[direction],
+            device_id_type=MESH,
+        )
+
+    def message(index, with_arrived):
+        distance = half_ring - (index + 1) // 2
+        for direction in range(2):
+            odd = lax.rem(index, 2)
+            token_half = odd if direction == 0 else 1 - odd
+            owner = tile_at(1 - direction, distance)
+            value = project(owner, pl.multiple_of(token_half * half, half), half)
+            if with_arrived:
+                message_copy(direction, index - 2).wait_recv()
+                value = value + in_msg[direction, index - 2].astype(jnp.float32)
+            out_msg[direction, index] = value.astype(jnp.bfloat16)
+            message_copy(direction, index).start()
+
+    messages = 2 * half_ring - 1
+
+    def first_messages(index, carry):
+        message(index, False)
+        return carry
+
+    def later_messages(index, carry):
+        message(index, True)
+        return carry
+
+    lax.fori_loop(0, 2, first_messages, 0)
+
+    for copy in sum_copies:
+        copy.wait_recv()
+    tile_sums = sums[...]
+    for offset in range(1, ys):
+        tile_sums = tile_sums + pair_sums[offset - 1]
+    ring_sums[0] = tile_sums
+    for offset in range(1, xs):
+        sum_copies.append(
+            pltpu.make_async_remote_copy(
+                src_ref=ring_sums.at[0],
+                dst_ref=ring_sums.at[offset],
+                send_sem=rsum_send.at[offset - 1],
+                recv_sem=rsum_recv.at[offset - 1],
+                device_id=device_at(lax.rem(tile + offset, xs), part),
+                device_id_type=MESH,
+            )
+        )
+        sum_copies[-1].start()
+
+    lax.fori_loop(2, messages, later_messages, 0)
+
+    own[...] = project(tile, 0, tokens)
+    for copy in sum_copies[ys - 1 :]:
+        copy.wait_recv()
+    all_sums = ring_sums[0]
+    for offset in range(1, xs):
+        all_sums = all_sums + ring_sums[offset]
+    inv_rms = lax.rsqrt(all_sums[0:1] / (feat * xs * ys) + 1e-05)
+    for index in range(messages - 2, messages):
+        for direction in range(2):
+            token_half = index % 2 if direction == 0 else 1 - index % 2
+            message_copy(direction, index).wait_recv()
+            own[token_half * half : (token_half + 1) * half, :] += in_msg[
+                direction, index
+            ].astype(jnp.float32)
+    qkv_out[...] = (own[...].T * inv_rms).astype(jnp.bfloat16)
+
+    for direction in range(2):
+        for item in range(arrivals):
+            gather_copy(direction, item, tile, 0, window(tile, 0)).wait_send()
+        for index in range(messages):
+            message_copy(direction, index).wait_send()
+    for copy in acc_copies + sum_copies:
+        copy.wait_send()
+    for outgoing, _ in feat_copies:
+        outgoing.wait_send()
+
+
+def fused(hidden, residual, w_down, gain, w_qkv):
+    gx = lax.axis_size("gx")
+    xs, ys = XS, gx // XS
+    rows, tokens = hidden.shape
+    feat = residual.shape[0]
+    cols = w_qkv.shape[2] // xs
+    cuts = next(c for c in (4, 2) if rows % (16 * c) == 0)
+    width = next(w for w in (512, 256, 128) if feat % w == 0)
+    arrivals = cuts * (xs // 2 - 1) + cuts // 2
+    messages = xs - 1
+    others = max(ys - 1, 1)
+    dma = pltpu.SemaphoreType.DMA
+    flops = 2 * tokens * (w_down.shape[1] * w_down.shape[2] + w_qkv.shape[1] * w_qkv.shape[2])
+    return pl.pallas_call(
+        functools.partial(fused_kernel, xs, ys, cuts, width),
+        out_shape=(
+            jax.ShapeDtypeStruct((feat, tokens), jnp.bfloat16),
+            jax.ShapeDtypeStruct((cols, tokens), jnp.bfloat16),
+        ),
+        in_specs=[
+            pl.BlockSpec(memory_space=pl.ANY),
+            pl.BlockSpec(memory_space=pl.ANY),
+            pl.BlockSpec(memory_space=pl.ANY),
+            pl.BlockSpec(memory_space=pltpu.VMEM),
+            pl.BlockSpec(memory_space=pl.ANY),
+        ],
+        out_specs=(
+            pl.BlockSpec(memory_space=pltpu.VMEM),
+            pl.BlockSpec(memory_space=pltpu.VMEM),
+        ),
+        scratch_shapes=[
+            pltpu.VMEM((xs, rows, tokens), jnp.bfloat16),
+            pltpu.VMEM((feat, tokens), jnp.bfloat16),
+            pltpu.VMEM((4, rows // cuts, ys * feat), jnp.bfloat16),
+            pltpu.VMEM((xs, ys * feat, cols), jnp.bfloat16),
+            pltpu.VMEM((ys, tokens, feat), jnp.float32),
+            pltpu.VMEM((others, tokens, feat), jnp.float32),
+            pltpu.VMEM((ys, tokens, feat), jnp.bfloat16),
+            pltpu.VMEM((8, tokens), jnp.float32),
+            pltpu.VMEM((others, 8, tokens), jnp.float32),
+            pltpu.VMEM((xs, 8, tokens), jnp.float32),
+            pltpu.VMEM((2, messages, tokens // 2, cols), jnp.bfloat16),
+            pltpu.VMEM((2, messages, tokens // 2, cols), jnp.bfloat16),
+            pltpu.VMEM((tokens, cols), jnp.float32),
+            dma((2,)),
+            dma((4,)),
+            dma((xs,)),
+            dma((2, arrivals)),
+            dma((2, arrivals)),
+            dma((others,)),
+            dma((others,)),
+            dma((others,)),
+            dma((others,)),
+            dma((others,)),
+            dma((others,)),
+            dma((xs - 1,)),
+            dma((xs - 1,)),
+            dma((2, messages)),
+            dma((2, messages)),
+        ],
+        compiler_params=pltpu.CompilerParams(
+            collective_id=0, has_side_effects=True, vmem_limit_bytes=66 * 10**6
+        ),
+        cost_estimate=pl.CostEstimate(
+            flops=flops,
+            bytes_accessed=2 * (w_down.size + w_qkv.size),
+            transcendentals=0,
+        ),
+    )(hidden, residual, w_down[0], gain[None, :], w_qkv[0])
+
+
+def on_device(hidden, residual, w_down, gain, w_qkv):
+    cols = w_qkv.shape[2] // XS
+    aligned = (
+        hidden.shape[0] % 32 == 0
+        and hidden.shape[1] % 32 == 0
+        and residual.shape[0] % 128 == 0
+        and cols % 128 == 0
+    )
+    step = fused if aligned else permuted
+    return step(hidden, residual, w_down, gain, w_qkv)
+
+
 def solution(mesh):
     placed = (
         P("gx", "groups"),

time: 850 us -> 209 us (0.25)
  waiting for transfers between devices: 697 us -> 0 us
  Pallas kernels: 0 us -> 203 us
  matrix products: 66.1 us -> 0 us
  local copies, waits for them, and re-layouts: 43 us -> 5.23 us
  other arithmetic: 29.3 us -> 0 us
  starting transfers between devices: 12.9 us -> 0 us
    ppermute x12 -> x0, waiting for transfers between devices: 697 us -> none  [swapped(): return lax.ppermute(block, axis, route)]
    pallas_call x0 -> x1, Pallas kernels: none -> 203 us  [fused(): pl.pallas_call(functools.partial(fused_kernel, xs, ys, cuts, width), out_...]
    dot_general x2 -> x0, matrix products: 66.1 us -> none  [the longest x1 51.4 us: on_device(): lax.dot_general(tile_down, gathered, (((0,), (0,)), ((), ())), preferred_...]
    dynamic_slice x6 -> x0, local copies, waits for them, and re-layouts: 21 us -> none  [the longest x4 11.3 us: halve_bits(): lax.dynamic_index_in_dim(shaped, high_bit, axis_pos, keepdims=False)]
    select_n x2 -> x0, other arithmetic: 18.3 us -> none  [collect_bits(): jnp.where(high_bit, jnp.concatenate([their_part, own_part], 0), jnp.conca...]
    reshape x2 -> x0, local copies, waits for them, and re-layouts: 15.5 us -> none  [halve_bits(): partial_value.reshape((2,) * bit_count + (partial_value.shape[0] // 2 **...]
    ppermute x12 -> x0, starting transfers between devices: 12.9 us -> none  [swapped(): return lax.ppermute(block, axis, route)]
  transfers between devices with their start and end apart: 12 -> 0, of which waited for: 11 -> 0; matrix products, arithmetic and copies ran while one was open for 1% -> 0% of each run, Pallas kernels for 0% -> 0%
where the time goes in v1:
time: 209 us; the launch traced here: 208 us
  Pallas kernels  203 us (97%)
  local copies, waits for them, and re-layouts  5.23 us (3%)
    pallas_call x1, Pallas kernels, fused(): pl.pallas_call(functools.partial(fused_kernel, xs, ys, cuts, width), out_...  203 us

profile of v1, /device:TPU:0, one launch (start us, length us, event | category | flops | bytes accessed | tf_op | source)
XLA Modules:
  0.0 208.4 jit_solution(6860269207817373637)
XLA Ops:
  0.6 1.3 broadcast_in_dim.3.gain
  1.9 202.5 %shard_map.68 = (bf16[1024,384]{1,0:T(8,128)(2,1)}, bf16[640,384]{1,0:T(8,128)(2,1)}) custom-call(bf16[2496,384]{1,0:T(8,128)(2,1)} %hidden.1, bf16[1024,384]{1,0:T(8,128)(2,1)} %residual.1, bf16[19968,2048]{1,0:T(8,128)(2,1)} %bitcast.w_down, bf16[1,1024]{1,0:T(2,128)(2,1)} %broadcast_in_dim.3.gain, bf16[2048,5120]{1,0:T(8,128)(2,1)} %bitcast.2), custom_call_target="tpu_custom_call" | custom-call | flops 39460012032 | bytes 102760448 | tf_op jit(solution)/shard_map/pallas_call | solution.py:501
  204.5 2.1 %copy.9 = bf16[1024,384]{1,0:T(8,128)(2,1)} copy(bf16[1024,384]{1,0:T(8,128)(2,1)} %get-tuple-element.4) | data formatting | bytes 1572864
  206.6 1.9 copy.10

commit v2 on v1

--- a/solution.py
+++ b/solution.py
@@ -237,12 +237,16 @@
     pl.semaphore_wait(barrier, xs - 1 + ys - 1)
 
     arrivals = cuts * (half_ring - 1) + cuts // 2
-    for item in range(cuts):
+
+
+    def send_own(direction, item):
+        chunk = item if direction == 0 else cuts - 1 - item
+        start = pl.multiple_of(chunk * cut, cut)
+        gather_copy(direction, item, tile, chunk, hidden.at[pl.ds(start, cut)]).start()
+
+    for item in range(2):
         for direction in range(2):
-            chunk = item if direction == 0 else cuts - 1 - item
-            gather_copy(
-                direction, item, tile, chunk, hidden.at[pl.ds(chunk * cut, cut)]
-            ).start()
+            send_own(direction, item)
     own_copy = pltpu.make_async_copy(hidden, held.at[tile], local_sem.at[0])
     own_copy.start()
     res_copy = pltpu.make_async_copy(residual, res_buf, local_sem.at[1])
@@ -295,10 +299,15 @@
             gather_copy(direction, item, piece, chunk, window(piece, chunk)).wait_recv()
             if forward:
 
-                @pl.when(item + cuts < arrivals)
+                @pl.when(item + 2 < cuts)
                 def _():
+                    send_own(direction, item + 2)
+
+                @pl.when(jnp.logical_and(item + 2 >= cuts, item + 2 < arrivals))
+                def _():
+                    piece, chunk = arrival(direction, item + 2 - cuts)
                     gather_copy(
-                        direction, item + cuts, piece, chunk, window(piece, chunk)
+                        direction, item + 2, piece, chunk, window(piece, chunk)
                     ).start()
 
     def weights_of(item, slot):
@@ -328,43 +337,95 @@
     for offset in range(1, ys):
         other = lax.rem(part + offset, ys)
         add_block(other, other * feat, first, slot, second, slot + 1)
-        acc_copies.append(
-            pltpu.make_async_remote_copy(
-                src_ref=acc.at[other],
-                dst_ref=acc_in.at[offset - 1],
-                send_sem=acc_send.at[offset - 1],
-                recv_sem=acc_recv.at[offset - 1],
-                device_id=device_at(tile, other),
-                device_id_type=MESH,
-            )
-        )
-        acc_copies[-1].start()
-    add_block(part, part * feat, first, slot, second, slot + 1)
-    total = acc[part]
-    for copy in acc_copies:
-        copy.wait_recv()
-    for offset in range(1, ys):
-        total = total + acc_in[offset - 1]
-    values = total.astype(jnp.bfloat16).astype(jnp.float32)
-    acc[part] = values
-    feats[part] = (values * gain[...].astype(jnp.float32)).astype(jnp.bfloat16)
-    feat_copies = []
-    for offset in range(1, ys):
-        other = lax.rem(part + offset, ys)
-        feat_copies.append(
-            [
+        for side in range(2):
+            acc_copies.append(
                 pltpu.make_async_remote_copy(
-                    src_ref=feats.at[sender],
-                    dst_ref=feats.at[sender],
-                    send_sem=feat_send.at[offset - 1],
-                    recv_sem=feat_recv.at[offset - 1],
+                    src_ref=acc.at[other, pl.ds(side * half, half)],
+                    dst_ref=acc_in.at[offset - 1, pl.ds(side * half, half)],
+                    send_sem=acc_send.at[offset - 1, side],
+                    recv_sem=acc_recv.at[offset - 1, side],
                     device_id=device_at(tile, other),
                     device_id_type=MESH,
                 )
-                for sender in (part, lax.rem(part + ys - offset, ys))
-            ]
-        )
-        feat_copies[-1][0].start()
+            )
+            acc_copies[-1].start()
+    add_block(part, part * feat, first, slot, second, slot + 1)
+
+    def feat_copy(offset, side, sender):
+        return pltpu.make_async_remote_copy(
+            src_ref=feats.at[sender, pl.ds(side * half, half)],
+            dst_ref=feats.at[sender, pl.ds(side * half, half)],
+            send_sem=feat_send.at[offset - 1, side],
+            recv_sem=feat_recv.at[offset - 1, side],
+            device_id=device_at(tile, lax.rem(part + offset, ys)),
+            device_id_type=MESH,
+        )
+
+    for side in range(2):
+        span = slice(side * half, (side + 1) * half)
+        total = acc[part, span, :]
+        for offset in range(1, ys):
+            acc_copies[2 * (offset - 1) + side].wait_recv()
+            total = total + acc_in[offset - 1, span, :]
+        values = total.astype(jnp.bfloat16).astype(jnp.float32)
+        acc[part, span, :] = values
+        feats[part, span, :] = (values * gain[...].astype(jnp.float32)[None, :]).astype(jnp.bfloat16)
+        for offset in range(1, ys):
+            feat_copy(offset, side, part).start()
+
+    def wait_feats(side):
+        for offset in range(1, ys):
+            feat_copy(offset, side, lax.rem(part + ys - offset, ys)).wait_recv()
+
+    def project(owner, start, size):
+        result = jnp.dot(
+            feats[0, pl.ds(start, size), :],
+            qkv_buf[owner, :feat, :],
+            preferred_element_type=jnp.float32,
+        )
+        for block in range(1, ys):
+            result = result + jnp.dot(
+                feats[block, pl.ds(start, size), :],
+                qkv_buf[owner, block * feat : (block + 1) * feat, :],
+                preferred_element_type=jnp.float32,
+            )
+        return result
+
+    def message_copy(direction, index):
+        return pltpu.make_async_remote_copy(
+            src_ref=out_msg.at[direction, index],
+            dst_ref=in_msg.at[direction, index],
+            send_sem=msg_send.at[direction, index],
+            recv_sem=msg_recv.at[direction, index],
+            device_id=ahead[direction],
+            device_id_type=MESH,
+        )
+
+    def message(index, with_arrived, first=False):
+        distance = half_ring - (index + 1) // 2
+        for direction in range(2):
+            if first:
+                wait_feats(direction)
+            odd = lax.rem(index, 2)
+            token_half = odd if direction == 0 else 1 - odd
+            owner = tile_at(1 - direction, distance)
+            value = project(owner, pl.multiple_of(token_half * half, half), half)
+            if with_arrived:
+                message_copy(direction, index - 2).wait_recv()
+                value = value + in_msg[direction, index - 2].astype(jnp.float32)
+            out_msg[direction, index] = value.astype(jnp.bfloat16)
+            message_copy(direction, index).start()
+
+    messages = 2 * half_ring - 1
+
+    def later_messages(index, carry):
+        message(index, True)
+        return carry
+
+    for owner in range(xs):
+        qkv_copy(owner).wait()
+    message(0, False, True)
+    message(1, False)
 
     upright = acc[part].T
     stream_out[...] = upright.astype(jnp.bfloat16)
@@ -382,60 +443,7 @@
             )
         )
         sum_copies[-1].start()
-
-    for owner in range(xs):
-        qkv_copy(owner).wait()
-    for _, incoming in feat_copies:
-        incoming.wait_recv()
-
-    def project(owner, start, size):
-        result = jnp.dot(
-            feats[0, pl.ds(start, size), :],
-            qkv_buf[owner, :feat, :],
-            preferred_element_type=jnp.float32,
-        )
-        for block in range(1, ys):
-            result = result + jnp.dot(
-                feats[block, pl.ds(start, size), :],
-                qkv_buf[owner, block * feat : (block + 1) * feat, :],
-                preferred_element_type=jnp.float32,
-            )
-        return result
-
-    def message_copy(direction, index):
-        return pltpu.make_async_remote_copy(
-            src_ref=out_msg.at[direction, index],
-            dst_ref=in_msg.at[direction, index],
-            send_sem=msg_send.at[direction, index],
-            recv_sem=msg_recv.at[direction, index],
-            device_id=ahead[direction],
-            device_id_type=MESH,
-        )
-
-    def message(index, with_arrived):
-        distance = half_ring - (index + 1) // 2
-        for direction in range(2):
-            odd = lax.rem(index, 2)
-            token_half = odd if direction == 0 else 1 - odd
-            owner = tile_at(1 - direction, distance)
-            value = project(owner, pl.multiple_of(token_half * half, half), half)
-            if with_arrived:
-                message_copy(direction, index - 2).wait_recv()
-                value = value + in_msg[direction, index - 2].astype(jnp.float32)
-            out_msg[direction, index] = value.astype(jnp.bfloat16)
-            message_copy(direction, index).start()
-
-    messages = 2 * half_ring - 1
-
-    def first_messages(index, carry):
-        message(index, False)
-        return carry
-
-    def later_messages(index, carry):
-        message(index, True)
-        return carry
-
-    lax.fori_loop(0, 2, first_messages, 0)
+    lax.fori_loop(2, messages - 3, later_messages, 0)
 
     for copy in sum_copies:
         copy.wait_recv()
@@ -456,7 +464,7 @@
         )
         sum_copies[-1].start()
 
-    lax.fori_loop(2, messages, later_messages, 0)
+    lax.fori_loop(messages - 3, messages, later_messages, 0)
 
     own[...] = project(tile, 0, tokens)
     for copy in sum_copies[ys - 1 :]:
@@ -481,8 +489,9 @@
             message_copy(direction, index).wait_send()
     for copy in acc_copies + sum_copies:
         copy.wait_send()
-    for outgoing, _ in feat_copies:
-        outgoing.wait_send()
+    for offset in range(1, ys):
+        for side in range(2):
+            feat_copy(offset, side, part).wait_send()
 
 
 def fused(hidden, residual, w_down, gain, w_qkv):
@@ -491,7 +500,7 @@
     rows, tokens = hidden.shape
     feat = residual.shape[0]
     cols = w_qkv.shape[2] // xs
-    cuts = next(c for c in (4, 2) if rows % (16 * c) == 0)
+    cuts = next(c for c in (6, 4, 2) if rows % (16 * c) == 0)
     width = next(w for w in (512, 256, 128) if feat % w == 0)
     arrivals = cuts * (xs // 2 - 1) + cuts // 2
     messages = xs - 1
@@ -534,10 +543,10 @@
             dma((xs,)),
             dma((2, arrivals)),
             dma((2, arrivals)),
-            dma((others,)),
-            dma((others,)),
-            dma((others,)),
-            dma((others,)),
+            dma((others, 2)),
+            dma((others, 2)),
+            dma((others, 2)),
+            dma((others, 2)),
             dma((others,)),
             dma((others,)),
             dma((xs - 1,)),
@@ -553,7 +562,7 @@
             bytes_accessed=2 * (w_down.size + w_qkv.size),
             transcendentals=0,
         ),
-    )(hidden, residual, w_down[0], gain[None, :], w_qkv[0])
+    )(hidden, residual, w_down[0], gain, w_qkv[0])
 
 
 def on_device(hidden, residual, w_down, gain, w_qkv):

time: 209 us -> 207 us (level)
  no operation moved by 1% of the time
where the time goes in v2:
time: 207 us; the launch traced here: 206 us
  Pallas kernels  202 us (98%)
  local copies, waits for them, and re-layouts  3.95 us (2%)
    pallas_call x1, Pallas kernels, fused(): pl.pallas_call(functools.partial(fused_kernel, xs, ys, cuts, width), out_...  202 us

profile of v2, /device:TPU:0, one launch (start us, length us, event | category | flops | bytes accessed | tf_op | source)
XLA Modules:
  0.0 206.4 jit_solution(9797490277122837306)
XLA Ops:
  0.6 201.8 %shard_map.68 = (bf16[1024,384]{1,0:T(8,128)(2,1)}, bf16[640,384]{1,0:T(8,128)(2,1)}) custom-call(bf16[2496,384]{1,0:T(8,128)(2,1)} %hidden.1, bf16[1024,384]{1,0:T(8,128)(2,1)} %residual.1, bf16[19968,2048]{1,0:T(8,128)(2,1)} %bitcast.w_down, bf16[1024]{0:T(1024)(128)(2,1)} %gain.1, bf16[2048,5120]{1,0:T(8,128)(2,1)} %bitcast.2), custom_call_target="tpu_custom_call" | custom-call | flops 39460012032 | bytes 102760448 | tf_op jit(solution)/shard_map/pallas_call | solution.py:510
  202.5 2.1 %copy.9 = bf16[1024,384]{1,0:T(8,128)(2,1)} copy(bf16[1024,384]{1,0:T(8,128)(2,1)} %get-tuple-element.4) | data formatting | bytes 1572864
  204.6 1.9 copy.10

commit v3 on v2

--- a/solution.py
+++ b/solution.py
@@ -428,7 +428,9 @@
     message(1, False)
 
     upright = acc[part].T
-    stream_out[...] = upright.astype(jnp.bfloat16)
+    res_buf[...] = upright.astype(jnp.bfloat16)
+    stream_copy = pltpu.make_async_copy(res_buf, stream_out, local_sem.at[2])
+    stream_copy.start()
     sums[...] = jnp.broadcast_to(jnp.sum(upright * upright, axis=0, keepdims=True), sums.shape)
     sum_copies = []
     for offset in range(1, ys):
@@ -489,9 +491,31 @@
             message_copy(direction, index).wait_send()
     for copy in acc_copies + sum_copies:
         copy.wait_send()
+    stream_copy.wait()
     for offset in range(1, ys):
         for side in range(2):
             feat_copy(offset, side, part).wait_send()
+
+
+def hand_over_kernel(stream, qkv, stream_out, qkv_out, sem):
+    moves = [
+        pltpu.make_async_copy(source, target, sem.at[lane])
+        for lane, (source, target) in enumerate(((stream, stream_out), (qkv, qkv_out)))
+    ]
+    for move in moves:
+        move.start()
+    for move in moves:
+        move.wait()
+
+
+def hand_over(stream, qkv):
+    return pl.pallas_call(
+        hand_over_kernel,
+        out_shape=tuple(jax.ShapeDtypeStruct(a.shape, a.dtype) for a in (stream, qkv)),
+        in_specs=[pl.BlockSpec(memory_space=pltpu.VMEM)] * 2,
+        out_specs=(pl.BlockSpec(memory_space=pl.ANY),) * 2,
+        scratch_shapes=[pltpu.SemaphoreType.DMA((2,))],
+    )(stream, qkv)
 
 
 def fused(hidden, residual, w_down, gain, w_qkv):
@@ -507,7 +531,7 @@
     others = max(ys - 1, 1)
     dma = pltpu.SemaphoreType.DMA
     flops = 2 * tokens * (w_down.shape[1] * w_down.shape[2] + w_qkv.shape[1] * w_qkv.shape[2])
-    return pl.pallas_call(
+    results = pl.pallas_call(
         functools.partial(fused_kernel, xs, ys, cuts, width),
         out_shape=(
             jax.ShapeDtypeStruct((feat, tokens), jnp.bfloat16),
@@ -521,7 +545,7 @@
             pl.BlockSpec(memory_space=pl.ANY),
         ],
         out_specs=(
-            pl.BlockSpec(memory_space=pltpu.VMEM),
+            pl.BlockSpec(memory_space=pl.ANY),
             pl.BlockSpec(memory_space=pltpu.VMEM),
         ),
         scratch_shapes=[
@@ -538,7 +562,7 @@
             pltpu.VMEM((2, messages, tokens // 2, cols), jnp.bfloat16),
             pltpu.VMEM((2, messages, tokens // 2, cols), jnp.bfloat16),
             pltpu.VMEM((tokens, cols), jnp.float32),
-            dma((2,)),
+            dma((3,)),
             dma((4,)),
             dma((xs,)),
             dma((2, arrivals)),
@@ -563,6 +587,7 @@
             transcendentals=0,
         ),
     )(hidden, residual, w_down[0], gain, w_qkv[0])
+    return hand_over(*results)
 
 
 def on_device(hidden, residual, w_down, gain, w_qkv):

time: 207 us -> 205 us (level)
  local copies, waits for them, and re-layouts: 3.95 us -> 0 us
    unnamed x2 -> x0, local copies, waits for them, and re-layouts: 3.95 us -> none
    pallas_call x0 -> x1, Pallas kernels: none -> 2.32 us  [hand_over(): pl.pallas_call(hand_over_kernel, out_shape=tuple((jax.ShapeDtypeStruct(a....]
where the time goes in v3:
time: 205 us
  Pallas kernels  204 us (100%)
    pallas_call x1, Pallas kernels, fused(): pl.pallas_call(functools.partial(fused_kernel, xs, ys, cuts, width), out_...  202 us

profile of v3, /device:TPU:0, one launch (start us, length us, event | category | flops | bytes accessed | tf_op | source)
XLA Modules:
  0.0 204.5 jit_solution(5808123205856886985)
XLA Ops:
  0.6 201.6 %shard_map.68 = (bf16[1024,384]{1,0:T(8,128)(2,1)}, bf16[640,384]{1,0:T(8,128)(2,1)}) custom-call(bf16[2496,384]{1,0:T(8,128)(2,1)} %hidden.1, bf16[1024,384]{1,0:T(8,128)(2,1)} %residual.1, bf16[19968,2048]{1,0:T(8,128)(2,1)} %bitcast.w_down, bf16[1024]{0:T(1024)(128)(2,1)} %gain.1, bf16[2048,5120]{1,0:T(8,128)(2,1)} %bitcast.2), custom_call_target="tpu_custom_call" | custom-call | flops 39460012032 | bytes 102760448 | tf_op jit(solution)/shard_map/pallas_call | solution.py:534
  202.2 2.3 %shard_map.69 = (bf16[1024,384]{1,0:T(8,128)(2,1)}, bf16[640,384]{1,0:T(8,128)(2,1)}) custom-call(bf16[1024,384]{1,0:T(8,128)(2,1)} %get-tuple-element.4.stream, bf16[640,384]{1,0:T(8,128)(2,1)} %get-tuple-element.5.qkv), custom_call_target="tpu_custom_call" | custom-call | tf_op jit(solution)/shard_map/pallas_call | solution.py:512

commit v4 on v3

--- a/solution.py
+++ b/solution.py
@@ -244,7 +244,8 @@
         start = pl.multiple_of(chunk * cut, cut)
         gather_copy(direction, item, tile, chunk, hidden.at[pl.ds(start, cut)]).start()
 
-    for item in range(2):
+    ahead_by = min(3, cuts)
+    for item in range(ahead_by):
         for direction in range(2):
             send_own(direction, item)
     own_copy = pltpu.make_async_copy(hidden, held.at[tile], local_sem.at[0])
@@ -299,15 +300,15 @@
             gather_copy(direction, item, piece, chunk, window(piece, chunk)).wait_recv()
             if forward:
 
-                @pl.when(item + 2 < cuts)
+                @pl.when(item + ahead_by < cuts)
                 def _():
-                    send_own(direction, item + 2)
-
-                @pl.when(jnp.logical_and(item + 2 >= cuts, item + 2 < arrivals))
+                    send_own(direction, item + ahead_by)
+
+                @pl.when(jnp.logical_and(item + ahead_by >= cuts, item + ahead_by < arrivals))
                 def _():
-                    piece, chunk = arrival(direction, item + 2 - cuts)
+                    piece, chunk = arrival(direction, item + ahead_by - cuts)
                     gather_copy(
-                        direction, item + 2, piece, chunk, window(piece, chunk)
+                        direction, item + ahead_by, piece, chunk, window(piece, chunk)
                     ).start()
 
     def weights_of(item, slot):

time: 205 us -> 205 us (level)
  no operation moved by 1% of the time
where the time goes in v4:
time: 205 us
  Pallas kernels  204 us (100%)
    pallas_call x1, Pallas kernels, fused(): pl.pallas_call(functools.partial(fused_kernel, xs, ys, cuts, width), out_...  202 us

profile of v4, /device:TPU:0, one launch (start us, length us, event | category | flops | bytes accessed | tf_op | source)
XLA Modules:
  0.0 204.5 jit_solution(7889343315144843861)
XLA Ops:
  0.6 201.6 %shard_map.68 = (bf16[1024,384]{1,0:T(8,128)(2,1)}, bf16[640,384]{1,0:T(8,128)(2,1)}) custom-call(bf16[2496,384]{1,0:T(8,128)(2,1)} %hidden.1, bf16[1024,384]{1,0:T(8,128)(2,1)} %residual.1, bf16[19968,2048]{1,0:T(8,128)(2,1)} %bitcast.w_down, bf16[1024]{0:T(1024)(128)(2,1)} %gain.1, bf16[2048,5120]{1,0:T(8,128)(2,1)} %bitcast.2), custom_call_target="tpu_custom_call" | custom-call | flops 39460012032 | bytes 102760448 | tf_op jit(solution)/shard_map/pallas_call | solution.py:535
  202.2 2.3 %shard_map.69 = (bf16[1024,384]{1,0:T(8,128)(2,1)}, bf16[640,384]{1,0:T(8,128)(2,1)}) custom-call(bf16[1024,384]{1,0:T(8,128)(2,1)} %get-tuple-element.4.stream, bf16[640,384]{1,0:T(8,128)(2,1)} %get-tuple-element.5.qkv), custom_call_target="tpu_custom_call" | custom-call | tf_op jit(solution)/shard_map/pallas_call | solution.py:513
